TPU v7x, 32 devices: a whole 2x2x4 slice. The times are simulated.
32 devices in a mesh: groups: 2 (over y), row: 4 (over z), col: 4 (over x, core).
Axes of the slice: x: 2, y: 2, z: 4, core: 2. Of those that a mesh axis runs over, the one named last changes fastest.
Arguments:
- raw_files: bfloat16 [128, 4, 8, 12000], P(('groups', 'row'), 'col'), parts along dimension 0
- file_channels: int32 [128, 4], P(('groups', 'row'), 'col'), parts along dimension 0, may hold values from 0 to 255, as said below
- reader_counts: int32 [8, 4], P(('groups', 'row'), 'col'), parts along dimension 0, may hold values from 0 to 16, as said below
- fir_taps: float32 [32], replicated, may hold values from -1 to 1
- band_bins: int32 [64], replicated, may hold values from 1 to 1499, as said below
Outputs:
- stack: bfloat16 [512, 4, 64, 128], P(('groups', 'row'), 'col'), parts along dimension 0
There are 2 independent parts, one for each index of `groups`. A program takes and returns all parts, laid end to end along the dimension named above; an argument that names none is the same for every part. Nothing has to cross between parts.
Inputs may be any that keep to these rules, and one draw needn't show every extreme that they name: `file_channels`: channel q belongs to owner row q // 64, column (q // 16) % 4. Every channel stands in exactly one live slot (slot below its reader's count), of a reader in its owner's column. Live slots of one reader name at most 4 channels of one owner; in every column some reader holds exactly 4 channels of every owner. Slots at or above the count hold arbitrary channel numbers. `reader_counts`: in every column some reader holds 16 live slots. `band_bins`: Distinct.
All inputs are finite; a program needn't handle non-finite values.
Results may differ from a plain program's by a relative error of at most 0.017.
Values may be sent and summed in bfloat16 or wider, within the bound.
A program may use at most 64 MiB of HBM per device.

v0:
```python
import math

import jax
import jax.numpy as jnp
from jax import lax
from jax.sharding import PartitionSpec as P

CH_DEV = 16
DEC = 4


def decimate(signal, fir_taps):
    count, records, samples = signal.shape
    length = samples // DEC
    taps = fir_taps.shape[0]
    outputs = 128
    span = outputs * DEC
    blocks = (length + outputs - 1) // outputs
    total = (blocks + 1) * span
    padded = jnp.pad(signal, ((0, 0), (0, 0), (0, total - samples)))
    leading = padded[:, :, : blocks * span].reshape(count, records, blocks, span)
    following = padded[:, :, span:].reshape(count, records, blocks, span)[:, :, :, : taps - DEC]
    window = jnp.concatenate([leading, following], axis=3)
    positions = jnp.arange(span + taps - DEC, dtype=jnp.int32)[:, None]
    columns = jnp.arange(outputs, dtype=jnp.int32)[None, :]
    offset = positions - DEC * columns
    banded = jnp.zeros((span + taps - DEC, outputs), jnp.float32)
    for index in range(taps):
        banded = banded + jnp.where(offset == index, fir_taps[index], jnp.float32(0.0))
    upper = banded.astype(jnp.bfloat16)
    lower = (banded - upper.astype(jnp.float32)).astype(jnp.bfloat16)
    result = jnp.einsum("iqbw,wn->iqbn", window, upper, preferred_element_type=jnp.float32)
    result = result + jnp.einsum("iqbw,wn->iqbn", window, lower, preferred_element_type=jnp.float32)
    return result.reshape(count, records, blocks * outputs)[:, :, :length].astype(jnp.bfloat16)


def whiten(signal, fir_taps, band_bins):
    count, records, samples = signal.shape
    length = samples // DEC
    decimated = decimate(signal, fir_taps)
    steps = jnp.arange(length, dtype=jnp.int32)
    product = band_bins[None, :] * steps[:, None] % length
    angle = 2.0 * math.pi / length * product.astype(jnp.float32)
    table = jnp.concatenate([jnp.cos(angle), -jnp.sin(angle)], axis=1).astype(jnp.bfloat16)
    spectra = jnp.dot(
        decimated.reshape(count * records, length), table, preferred_element_type=jnp.float32
    )
    power = jnp.mean(spectra * spectra, axis=1, keepdims=True)
    white = spectra / jnp.sqrt(power + 1e-06)
    return white.reshape(count, records, table.shape[1]).astype(jnp.bfloat16)


def slot_plan(file_channels, reader_counts, nrows, ncols, capacity):
    channels = file_channels[:, 0]
    slots = channels.shape[0]
    order = jnp.arange(slots, dtype=jnp.int32)
    live = order < reader_counts[0, 0]
    owner = channels // (CH_DEV * ncols)
    place = channels % CH_DEV
    earlier = (owner[None, :] == owner[:, None]) & live[None, :] & (order[None, :] < order[:, None])
    rank = jnp.sum(earlier.astype(jnp.int32), axis=1)
    where_to = jnp.where(live, owner * capacity + rank, -1)
    target = jnp.arange(nrows * capacity, dtype=jnp.int32)
    match = (where_to[None, :] == target[:, None]).astype(jnp.int32)
    filled = jnp.sum(match, axis=1) > 0
    source = jnp.sum(match * order[None, :], axis=1)
    label = jnp.where(filled, jnp.sum(match * place[None, :], axis=1), -1)
    return (source, filled, label)


def pack(data, source, filled, nrows, capacity):
    chosen = jnp.where(filled[:, None, None], data[source], jnp.zeros((), data.dtype))
    return chosen.reshape((nrows, capacity) + data.shape[1:])


def settle(received, labels):
    flat = received.reshape((-1,) + received.shape[2:])
    marks = labels.reshape(-1).astype(jnp.int32)
    total = marks.shape[0]
    match = (marks[None, :] == jnp.arange(CH_DEV, dtype=jnp.int32)[:, None]).astype(jnp.int32)
    source = jnp.sum(match * jnp.arange(total, dtype=jnp.int32)[None, :], axis=1)
    return flat[source]


def on_device(raw_files, file_channels, reader_counts, fir_taps, band_bins):
    nrows = lax.axis_size("row")
    ncols = lax.axis_size("col")
    capacity = max(2, (CH_DEV + nrows - 1) // nrows)
    source, filled, label = slot_plan(file_channels, reader_counts, nrows, ncols, capacity)
    labels = label.reshape(nrows, capacity).astype(jnp.bfloat16)
    reader_white = whiten(raw_files[:, 0], fir_taps, band_bins)
    outgoing = pack(reader_white, source, filled, nrows, capacity)
    arrived, arrived_labels = (
        lax.all_to_all(outgoing, "row", split_axis=0, concat_axis=0, tiled=True),
        lax.all_to_all(labels, "row", split_axis=0, concat_axis=0, tiled=True),
    )
    white_own = settle(arrived, arrived_labels)
    records = white_own.shape[1]
    width = white_own.shape[2] // 2
    row_white = lax.all_gather(white_own, "col", axis=0, tiled=True)
    left_count = row_white.shape[0]
    left = (
        row_white.reshape(left_count, records, 2, width)
        .transpose(0, 2, 1, 3)
        .reshape(left_count, 2 * records, width)
    )
    piece = lax.all_gather(white_own, "row", axis=0, tiled=True)
    right_count = piece.shape[0]
    split_piece = piece.reshape(right_count, records, 2, width)
    piece_re = split_piece[:, :, 0, :]
    piece_im = split_piece[:, :, 1, :]
    right_real = jnp.concatenate([piece_re, piece_im], axis=1)
    right_imag = jnp.concatenate([-piece_im, piece_re], axis=1)
    real = jnp.einsum("ikb,jkb->ijb", left, right_real, preferred_element_type=jnp.float32)
    imag = jnp.einsum("ikb,jkb->ijb", left, right_imag, preferred_element_type=jnp.float32)
    stacked = (jnp.concatenate([real, imag], axis=2) / records).astype(jnp.bfloat16)
    return stacked[:, None, :, :]


def solution(mesh):
    return jax.shard_map(
        on_device,
        mesh=mesh,
        in_specs=(
            P(("groups", "row"), "col", None, None),
            P(("groups", "row"), "col"),
            P(("groups", "row"), "col"),
            P(),
            P(),
        ),
        out_specs=P(("groups", "row"), "col", None, None),
        check_vma=False,
    )
```

profile of v0, /device:TPU:0, one launch (start us, length us, event | category | flops | bytes accessed | tf_op | source)
XLA Modules:
  0.0 111.3 jit_solution(5888975628344206008)
XLA Ops:
  0.0 0.7 and_select_fusion.2
  0.7 0.7 fusion.64
  2.0 0.2 convert_reduce_fusion.1
  2.2 0.1 select_reduce_fusion.1
  2.3 0.7 convert_element_type.76
  3.0 6.3 %all-to-all-start.1 = ((bf16[4,1,4]{2,1,0:T(2,128)(2,1)}), bf16[4,1,4]{2,1,0:T(2,128)(2,1)S(1)}, u32[]{:S(2)}, u32[]{:S(2)}) async-start(bf16[4,1,4]{2,1,0:T(2,128)(2,1)} %convert_element_type.76), calls=%async_computation.1 | async-start | bytes 4096 | tf_op jit(solution)/shard_map/all_to_all | solution.py:95
  9.4 2.1 %fusion.137 = (f32[1]{0:T(128)}, f32[1]{0:T(128)}, f32[1]{0:T(128)}, f32[1]{0:T(128)}, f32[1]{0:T(128)}, /*index=5*/f32[1]{0:T(128)}, f32[1]{0:T(128)}, f32[1]{0...) fusion(f32[32]{0:T(128)} %param.8), kind=kLoop, calls=%fused_computation.186 | loop fusion | bytes 152 | tf_op jit(solution)/shard_map/slice | solution.py:29
  11.4 1.8 %fusion.138 = (f32[1]{0:T(128)}, f32[1]{0:T(128)}, f32[1]{0:T(128)}, f32[1]{0:T(128)}, f32[1]{0:T(128)}, /*index=5*/f32[1]{0:T(128)}, f32[1]{0:T(128)}, f32[1]{0...) fusion(f32[32]{0:T(128)} %param.8), kind=kLoop, calls=%fused_computation.187 | loop fusion | bytes 104 | tf_op jit(solution)/shard_map/slice | solution.py:29
  13.3 3.2 %pad_slice_fusion.1 = (bf16[16,8,12288]{2,1,0:T(8,128)(2,1)S(1)}, bf16[16,8,12288]{2,1,0:T(8,128)(2,1)S(1)}) fusion(bf16[16,8,12000]{2,1,0:T(8,128)(2,1)} %bitcast.115), kind=kLoop, calls=%fused_computation.6 | loop fusion | bytes 9363456 | tf_op jit(solution)/shard_map/slice | solution.py:21
  16.5 1.3 %copy.29 = bf16[16,8,24,512]{3,2,1,0:T(8,128)(2,1)S(1)} copy(bf16[16,8,24,512]{3,1,2,0:T(8,128)(2,1)S(1)} %bitcast.112) | data formatting | bytes 6291456
  17.8 0.1 slice.157
  17.9 1.3 %copy.30 = bf16[16,8,24,512]{3,2,1,0:T(8,128)(2,1)S(1)} copy(bf16[16,8,24,512]{3,1,2,0:T(8,128)(2,1)S(1)} %bitcast.111) | data formatting | bytes 6291456
  19.2 22.2 %fusion = f32[16,8,24,128]{3,2,1,0:T(8,128)S(1)} fusion(bf16[16,8,24,28]{3,2,1,0:T(8,128)(2,1)S(1)} %slice.157, bf16[16,8,24,512]{3,2,1,0:T(8,128)(2,1)S(1)} %copy.30, f32[]{:T(128)} %bitcast.35, f32[]{:T(128)} %bitcast.34, f32[]{:T(128)} %bitcast.33, f32[]{:T(128)} %bitcast.32, f32[]{:T(128)} %bitcast.31, f32[]{:T(128)} %bitcast.30, f32[]{:T(128)} %bitcast.29, ...), kind=kOutput, calls=%fused_computation.7 | convolution fusion | flops 438220800 | bytes 4891264 | tf_op jit(solution)/shard_map/iqbw,wn->iqbn/dot_general | solution.py:33
  41.4 22.0 %add_convert_fusion = bf16[16,8,24,128]{3,2,1,0:T(8,128)(2,1)S(1)} fusion(f32[16,8,24,128]{3,2,1,0:T(8,128)S(1)} %fusion, bf16[16,8,24,28]{3,2,1,0:T(8,128)(2,1)S(1)} %slice.157, bf16[16,8,24,512]{3,2,1,0:T(8,128)(2,1)S(1)} %copy.30, f32[]{:T(128)} %bitcast.35, f32[]{:T(128)} %bitcast.34, f32[]{:T(128)} %bitcast.33, f32[]{:T(128)} %bitcast.32, ...), kind=kOutput, calls=%fused_computation.11 | convolution fusion | flops 438799872 | bytes 5677696 | tf_op jit(solution)/shard_map/iqbw,wn->iqbn/dot_general | solution.py:32
  63.4 0.3 reshape.222
  63.7 3.6 %cosine_convert_fusion = (bf16[3000,64]{0,1:T(8,128)(2,1)S(1)}, bf16[3000,64]{0,1:T(8,128)(2,1)S(1)}) fusion(s32[64]{0:T(128)S(1)} %copy-done), kind=kLoop, calls=%fused_computation.21 | loop fusion | flops 2304000 | bytes 768256 | tf_op jit(solution)/shard_map/convert.1
  67.3 0.5 multiply_reduce_fusion
  68.0 0.6 gather_fusion
  68.6 0.7 broadcast_select_fusion
  69.3 5.1 %all-to-all-start = ((bf16[4,4,8,128]{3,2,1,0:T(8,128)(2,1)}), bf16[4,4,8,128]{3,2,1,0:T(8,128)(2,1)S(1)}, u32[]{:S(2)}, u32[]{:S(2)}) async-start(bf16[4,4,8,128]{3,2,1,0:T(8,128)(2,1)} %broadcast_select_fusion), calls=%async_computation | async-start | bytes 65536 | tf_op jit(solution)/shard_map/all_to_all | solution.py:94
  74.6 5.4 %all-to-all-done = bf16[4,4,8,128]{3,2,1,0:T(8,128)(2,1)S(1)} async-done(((bf16[4,4,8,128]{3,2,1,0:T(8,128)(2,1)}), bf16[4,4,8,128]{3,2,1,0:T(8,128)(2,1)S(1)}, u32[]{:S(2)}, u32[]{:S(2)}) %all-to-all-start) | async-done | bytes 32800 | tf_op jit(solution)/shard_map/all_to_all | solution.py:94
  80.0 0.6 gather_fusion.1
  80.6 13.3 %all-gather = bf16[64,8,128]{2,1,0:T(8,128)(2,1)S(1)} all-gather(bf16[16,8,128]{2,1,0:T(8,128)(2,1)S(1)} %gather_fusion.1), channel_id=2, replica_groups=mesh['groups'=2,'row'=4,'col'=4] {'row'}, dimensions={0}, use_global_device_ids=true | all-gather | bytes 163840 | tf_op jit(solution)/shard_map/all_gather | solution.py:107
  94.0 5.6 %all-gather.1 = bf16[64,8,128]{2,1,0:T(8,128)(2,1)S(1)} all-gather(bf16[16,8,128]{2,1,0:T(8,128)(2,1)S(1)} %gather_fusion.1), channel_id=3, replica_groups=mesh['groups'=2,'row'=4,'col'=4] {'col'}, dimensions={0}, use_global_device_ids=true | all-gather | bytes 163840 | tf_op jit(solution)/shard_map/all_gather | solution.py:100
  99.5 0.2 copy.19
  99.8 0.1 reshape.226
  100.0 0.4 copy.20
  100.3 0.5 fusion.44
  100.8 3.1 %copy.21 = f32[64,64,64]{0,1,2:T(8,128)} copy(f32[64,64,64]{2,1,0:T(8,128)S(1)} %fusion.44) | data formatting | bytes 2097152 | tf_op jit(solution)/shard_map/ikb,jkb->ijb/dot_general | solution.py:114
  103.9 0.5 fusion.48
  104.4 3.1 %copy.22 = f32[64,64,64]{0,1,2:T(8,128)} copy(f32[64,64,64]{2,1,0:T(8,128)S(1)} %fusion.48) | data formatting | bytes 2097152 | tf_op jit(solution)/shard_map/ikb,jkb->ijb/dot_general | solution.py:115
  107.5 3.8 %fusion.2 = bf16[64,1,64,128]{3,2,1,0:T(8,128)(2,1)} fusion(f32[64,1,64,64]{3,2,1,0:T(8,128)} %bitcast.114, f32[64,1,64,64]{3,2,1,0:T(8,128)} %bitcast.113), kind=kLoop, calls=%fused_computation.10 | loop fusion | flops 1572864 | bytes 3145728 | tf_op jit(solution)/shard_map/convert_element_type | solution.py:116
  (20 shorter events, 0.5 us)
Async XLA Ops:
  3.0 66.3 %all-to-all-start.1 = ((bf16[4,1,4]{2,1,0:T(2,128)(2,1)}), bf16[4,1,4]{2,1,0:T(2,128)(2,1)S(1)}, u32[]{:S(2)}, u32[]{:S(2)}) async-start(bf16[4,1,4]{2,1,0:T(2,128)(2,1)} %convert_element_type.76), calls=%async_computation.1 | async-start | bytes 4096 | tf_op jit(solution)/shard_map/all_to_all | solution.py:95
  41.4 22.4 %copy-start = (s32[64]{0:T(128)S(1)}, s32[64]{0:T(128)}, u32[]{:S(2)}) copy-start(s32[64]{0:T(128)} %param.9) | copy-start | bytes 772
  69.3 10.8 %all-to-all-start = ((bf16[4,4,8,128]{3,2,1,0:T(8,128)(2,1)}), bf16[4,4,8,128]{3,2,1,0:T(8,128)(2,1)S(1)}, u32[]{:S(2)}, u32[]{:S(2)}) async-start(bf16[4,4,8,128]{3,2,1,0:T(8,128)(2,1)} %broadcast_select_fusion), calls=%async_computation | async-start | bytes 65536 | tf_op jit(solution)/shard_map/all_to_all | solution.py:94
where the time goes:
time: 112 us; the launch traced here: 111 us
  matrix products  45.6 us (41%)
  local copies, waits for them, and re-layouts  19 us (17%)
  blocking collectives  18.9 us (17%)
  starting transfers between devices  11.4 us (10%)
  other arithmetic  10.1 us (9%)
  waiting for transfers between devices  5.41 us (5%)
    dot_general x1, matrix products, decimate(): jnp.einsum('iqbw,wn->iqbn', window, lower, preferred_element_type=jnp.flo...  22.2 us
    dot_general x1, matrix products, decimate(): jnp.einsum('iqbw,wn->iqbn', window, upper, preferred_element_type=jnp.flo...  22 us
    all_gather x1, blocking collectives, on_device(): piece = lax.all_gather(white_own, 'row', axis=0, tiled=True)  13.3 us
    all_to_all x1, starting transfers between devices, on_device(): lax.all_to_all(labels, 'row', split_axis=0, concat_axis=0, tiled=True)  6.32 us
    all_gather x1, blocking collectives, on_device(): row_white = lax.all_gather(white_own, 'col', axis=0, tiled=True)  5.59 us
    all_to_all x1, waiting for transfers between devices, on_device(): lax.all_to_all(outgoing, 'row', split_axis=0, concat_axis=0, tiled=True)  5.41 us
    all_to_all x1, starting transfers between devices, on_device(): lax.all_to_all(outgoing, 'row', split_axis=0, concat_axis=0, tiled=True)  5.09 us
    slice x2, local copies, waits for them, and re-layouts, decimate(): fir_taps[index]  3.9 us
  transfers between devices with their start and end apart: 2, of which 1 were waited for; matrix products, arithmetic and copies ran while one was open for 54% of the time, Pallas kernels for 0%

commit v1 on v0

v1 whole, which is shorter than its diff:
```python
import functools
import math

import jax
import jax.numpy as jnp
from jax import lax
from jax.experimental import pallas as pl
from jax.experimental.pallas import tpu as pltpu
from jax.sharding import PartitionSpec as P

CH_DEV = 16
DEC = 4
LANES = 128
SPAN = 512
PIECE = 2048
MESH = pl.DeviceIdType.MESH
F32 = jnp.float32
BF16 = jnp.bfloat16


def turn_cos(steps, period):
    rest = steps - period * jnp.floor(steps * (1.0 / period) + 0.5)
    y = (period / 4.0 - jnp.abs(rest)) * (2.0 * math.pi / period)
    z = y * y
    poly = -1.0 / 39916800.0
    for factor in (1.0 / 362880.0, -1.0 / 5040.0, 1.0 / 120.0, -1.0 / 6.0, 1.0):
        poly = poly * z + factor
    return poly * y


def gather_kernel(
    nrows, ncols, slots, records, samples, taps,
    x_hbm, chan_ref, count_ref, fir_ref, bins_ref,
    right_ref, left_ref,
    x_ref, table_ref, edge_ref, cos_ref, sin_ref, white_ref, col_ref, label_ref,
    load_sem, lsend, lrecv, rsend, rrecv, csend, crecv,
):
    me_row = lax.axis_index("row")
    me_col = lax.axis_index("col")
    barrier = pltpu.get_barrier_semaphore()
    for d in range(1, nrows):
        pl.semaphore_signal(barrier, inc=1, device_id={"row": lax.rem(me_row + d, nrows)}, device_id_type=MESH)
    for d in range(1, ncols):
        pl.semaphore_signal(barrier, inc=1, device_id={"col": lax.rem(me_col + d, ncols)}, device_id_type=MESH)

    pieces = [(s, min(PIECE, samples - s)) for s in range(0, samples, PIECE)]
    loads = []
    for n, (start, size) in enumerate(pieces):
        load = pltpu.make_async_copy(
            x_hbm.at[:, pl.ds(start, size)], x_ref.at[:, pl.ds(start, size)], load_sem.at[n]
        )
        load.start()
        loads.append(load)

    width = nrows * slots
    count = count_ref[0]
    lane = lax.broadcasted_iota(jnp.int32, (8, width), 1)
    label = jnp.full((8, width), -1, jnp.int32)
    for s in range(slots):
        channel = jnp.where(s < count, chan_ref[s], -1)
        label = jnp.where(lane == me_row * slots + s, channel, label)
    label_ref[me_row] = label

    pl.semaphore_wait(barrier, nrows - 1 + ncols - 1)
    label_copies = []
    for d in range(1, nrows):
        copy = pltpu.make_async_remote_copy(
            src_ref=label_ref.at[me_row], dst_ref=label_ref.at[me_row],
            send_sem=lsend.at[d], recv_sem=lrecv.at[d],
            device_id={"row": lax.rem(me_row + d, nrows)}, device_id_type=MESH,
        )
        copy.start()
        label_copies.append(copy)

    length = samples // DEC
    half = LANES // 2
    lane8 = lax.broadcasted_iota(jnp.int32, (8, LANES), 1)
    sub8 = lax.broadcasted_iota(jnp.int32, (8, LANES), 0)
    upper = lane8 >= half
    binlane = jnp.where(upper, lane8 - half, lane8)
    bins = jnp.zeros((8, LANES), jnp.int32)
    for k in range(half):
        bins = jnp.where(binlane == k, bins_ref[k], bins)
    bins = bins.astype(F32)
    quarter = length / 4.0
    off1 = jnp.where(upper, quarter, 0.0)
    off2 = jnp.where(upper, 2.0 * quarter, quarter)
    phase = sub8 % DEC
    later = sub8 // DEC
    groups = taps // DEC
    filt = []
    for i in range(groups):
        f = jnp.zeros((8, LANES), F32)
        for p in range(DEC):
            f = jnp.where(phase == p, fir_ref[DEC * i + p], f)
        filt.append(f)
    base1 = jnp.zeros((8, LANES), F32)
    base2 = jnp.zeros((8, LANES), F32)
    for i in range(groups):
        steps = bins * (later - i).astype(F32)
        base1 = base1 + filt[i] * turn_cos(steps + off1, length)
        base2 = base2 + filt[i] * turn_cos(steps + off2, length)
    turns = SPAN // 8
    hops = pl.cdiv(samples, SPAN)
    hop_rows = pl.cdiv(hops, 8) * 8
    for a in range(0, turns, 8):
        steps = bins * ((sub8 + a) * (8 // DEC)).astype(F32)
        cos_ref[pl.ds(a, 8), :] = turn_cos(steps, length)
        sin_ref[pl.ds(a, 8), :] = turn_cos(steps - quarter, length)
    for a in range(0, hop_rows, 8):
        steps = bins * ((sub8 + a) * (SPAN // DEC)).astype(F32)
        cos_ref[pl.ds(turns + a, 8), :] = turn_cos(steps, length)
        sin_ref[pl.ds(turns + a, 8), :] = turn_cos(steps - quarter, length)
    for a in range(0, turns, 2):
        one, two = [], []
        for b in (a, a + 1):
            c = cos_ref[pl.ds(b, 1), :]
            s = sin_ref[pl.ds(b, 1), :]
            one.append(c * base1 + s * base2)
            two.append(c * base2 - s * base1)
        table_ref[pl.ds(8 * a, 16), pl.ds(0, LANES)] = jnp.concatenate(one, axis=0).astype(BF16)
        table_ref[pl.ds(8 * a, 16), pl.ds(LANES, LANES)] = jnp.concatenate(two, axis=0).astype(BF16)
    per = 8 // DEC
    edge_ref[...] = jnp.zeros(edge_ref.shape, BF16)
    before = {}
    for dist in range(-(groups - 1), 0):
        n = later + dist
        before[dist] = jnp.where(n < 0, turn_cos(bins * n.astype(F32) + off1, length), 0.0)
    edges = pl.cdiv(taps, 16) * 2
    rows = []
    for a in range(edges):
        fix = jnp.zeros((8, LANES), F32)
        for i in range(groups):
            if per * a - i < 0:
                fix = fix - filt[i] * before[per * a - i]
        rows.append(fix)
    for a in range(0, edges, 2):
        edge_ref[pl.ds(8 * a, 16), :] = jnp.concatenate(rows[a:a + 2], axis=0).astype(BF16)

    count_rows = slots * records
    total = jnp.zeros((count_rows, LANES), F32)
    ready = 0
    for h in range(hops):
        start = h * SPAN
        size = min(SPAN, samples - start)
        while ready < len(pieces) and pieces[ready][0] < start + size:
            loads[ready].wait()
            ready += 1
        part = jnp.dot(x_ref[:, pl.ds(start, size)], table_ref[pl.ds(0, size), :], preferred_element_type=F32)
        c = cos_ref[pl.ds(turns + h, 1), :]
        s = sin_ref[pl.ds(turns + h, 1), :]
        total = total + part[:, :LANES] * c + part[:, LANES:] * s
    total = total + jnp.dot(x_ref[:, pl.ds(0, LANES)], edge_ref[...], preferred_element_type=F32)
    power = jnp.mean(total * total, axis=1, keepdims=True)
    white_ref[...] = total * lax.rsqrt(power + 1e-06)
    alive = lax.broadcasted_iota(jnp.int32, (slots, LANES), 0) < count
    for e in range(records):
        rows = white_ref[pl.ds(e, slots, stride=records), :]
        col_ref[me_row, e] = jnp.where(alive, rows, 0.0).astype(BF16)

    row_copies = []
    for d in range(1, nrows):
        copy = pltpu.make_async_remote_copy(
            src_ref=col_ref.at[me_row], dst_ref=col_ref.at[me_row],
            send_sem=rsend.at[d], recv_sem=rrecv.at[d],
            device_id={"row": lax.rem(me_row + d, nrows)}, device_id_type=MESH,
        )
        copy.start()
        row_copies.append(copy)
    for copy in label_copies:
        copy.wait()
    label = label_ref[0]
    for r in range(1, nrows):
        label = jnp.maximum(label, label_ref[r])
    channels = nrows * CH_DEV
    order = lax.broadcasted_iota(jnp.int32, (channels, width), 0)
    wanted = (order // CH_DEV) * (ncols * CH_DEV) + me_col * CH_DEV + order % CH_DEV
    pick = (wanted == label[0:1, :]).astype(F32).astype(BF16)
    for copy in row_copies:
        copy.wait()
    for e in range(records):
        rows = jnp.concatenate([col_ref[r, e] for r in range(nrows)], axis=0)
        right_ref[e] = jnp.dot(pick, rows, preferred_element_type=F32).astype(BF16)
    first = pl.multiple_of(me_row * CH_DEV, CH_DEV)
    for e in range(records):
        left_ref[me_col, e] = right_ref[e, pl.ds(first, CH_DEV), :]
    col_copies = []
    for d in range(1, ncols):
        copy = pltpu.make_async_remote_copy(
            src_ref=left_ref.at[me_col], dst_ref=left_ref.at[me_col],
            send_sem=csend.at[d], recv_sem=crecv.at[d],
            device_id={"col": lax.rem(me_col + d, ncols)}, device_id_type=MESH,
        )
        copy.start()
        col_copies.append(copy)
    for copy in col_copies:
        copy.wait()


def pair_kernel(records, left_ref, right_ref, out_ref, u1_ref, u2_ref, v1_ref, v2_ref):
    half = LANES // 2
    channels = right_ref.shape[1]

    @pl.when(pl.program_id(0) == 0)
    def _():
        upper = lax.broadcasted_iota(jnp.int32, (channels, LANES), 1) >= half
        for e in range(records):
            v = right_ref[e].astype(F32)
            w = pltpu.roll(v, half, 1)
            v1_ref[e] = jnp.where(upper, w, v)
            v2_ref[e] = jnp.where(upper, v, w)

    upper = lax.broadcasted_iota(jnp.int32, (CH_DEV, LANES), 1) >= half
    scale = 1.0 / records
    for e in range(records):
        u = left_ref[0, e].astype(F32) * scale
        w = pltpu.roll(u, half, 1)
        u1_ref[e] = u
        u2_ref[e] = jnp.where(upper, -w, w)

    @pl.loop(0, channels // 16)
    def _(jb):
        at = pl.ds(pl.multiple_of(jb * 16, 16), 16)
        v1 = [v1_ref[e, at, :] for e in range(records)]
        v2 = [v2_ref[e, at, :] for e in range(records)]
        for i in range(CH_DEV):
            total = u1_ref[0, pl.ds(i, 1), :] * v1[0] + u2_ref[0, pl.ds(i, 1), :] * v2[0]
            for e in range(1, records):
                total = total + u1_ref[e, pl.ds(i, 1), :] * v1[e]
                total = total + u2_ref[e, pl.ds(i, 1), :] * v2[e]
            out_ref[i, at, :] = total.astype(BF16)


def on_device(raw_files, file_channels, reader_counts, fir_taps, band_bins):
    nrows = lax.axis_size("row")
    ncols = lax.axis_size("col")
    slots, _, records, samples = raw_files.shape
    taps = fir_taps.shape[0]
    width = nrows * slots
    channels = nrows * CH_DEV
    signal = raw_files.reshape(slots * records, samples)
    hop_rows = pl.cdiv(pl.cdiv(samples, SPAN), 8) * 8
    tall = SPAN // 8 + hop_rows
    smem = pl.BlockSpec(memory_space=pltpu.SMEM)
    vmem = pl.BlockSpec(memory_space=pltpu.VMEM)
    right, left = pl.pallas_call(
        functools.partial(gather_kernel, nrows, ncols, slots, records, samples, taps),
        out_shape=(
            jax.ShapeDtypeStruct((records, channels, LANES), BF16),
            jax.ShapeDtypeStruct((ncols, records, CH_DEV, LANES), BF16),
        ),
        in_specs=[pl.BlockSpec(memory_space=pl.ANY), smem, smem, smem, smem],
        out_specs=(vmem, vmem),
        scratch_shapes=[
            pltpu.VMEM((slots * records, samples), BF16),
            pltpu.VMEM((SPAN, 2 * LANES), BF16),
            pltpu.VMEM((LANES, LANES), BF16),
            pltpu.VMEM((tall, LANES), F32),
            pltpu.VMEM((tall, LANES), F32),
            pltpu.VMEM((slots * records, LANES), F32),
            pltpu.VMEM((nrows, records, slots, LANES), BF16),
            pltpu.VMEM((nrows, 8, width), jnp.int32),
            pltpu.SemaphoreType.DMA((pl.cdiv(samples, PIECE),)),
            pltpu.SemaphoreType.DMA((nrows,)),
            pltpu.SemaphoreType.DMA((nrows,)),
            pltpu.SemaphoreType.DMA((nrows,)),
            pltpu.SemaphoreType.DMA((nrows,)),
            pltpu.SemaphoreType.DMA((ncols,)),
            pltpu.SemaphoreType.DMA((ncols,)),
        ],
        compiler_params=pltpu.CompilerParams(
            collective_id=0, has_side_effects=True, vmem_limit_bytes=40 * 2**20
        ),
    )(signal, file_channels.reshape(-1), reader_counts.reshape(-1), fir_taps, band_bins)
    stacked = pl.pallas_call(
        functools.partial(pair_kernel, records),
        grid=(ncols,),
        out_shape=jax.ShapeDtypeStruct((ncols * CH_DEV, channels, LANES), BF16),
        in_specs=[
            pl.BlockSpec((1, records, CH_DEV, LANES), lambda c: (c, 0, 0, 0)),
            pl.BlockSpec((records, channels, LANES), lambda c: (0, 0, 0)),
        ],
        out_specs=pl.BlockSpec((CH_DEV, channels, LANES), lambda c: (c, 0, 0)),
        scratch_shapes=[
            pltpu.VMEM((records, CH_DEV, LANES), F32),
            pltpu.VMEM((records, CH_DEV, LANES), F32),
            pltpu.VMEM((records, channels, LANES), F32),
            pltpu.VMEM((records, channels, LANES), F32),
        ],
        compiler_params=pltpu.CompilerParams(vmem_limit_bytes=40 * 2**20),
    )(left, right)
    return stacked[:, None, :, :]


def solution(mesh):
    return jax.shard_map(
        on_device,
        mesh=mesh,
        in_specs=(
            P(("groups", "row"), "col", None, None),
            P(("groups", "row"), "col"),
            P(("groups", "row"), "col"),
            P(),
            P(),
        ),
        out_specs=P(("groups", "row"), "col", None, None),
        check_vma=False,
    )
```

time: 112 us -> 23.4 us (0.21)
  matrix products: 45.6 us -> 0 us
  blocking collectives: 18.9 us -> 0 us
  Pallas kernels: 0 us -> 18.7 us
  local copies, waits for them, and re-layouts: 19 us -> 3.83 us
  starting transfers between devices: 11.4 us -> 0 us
  other arithmetic: 10.1 us -> 0 us
  waiting for transfers between devices: 5.41 us -> 0 us
    dot_general x5 -> x0, matrix products: 45.6 us -> none  [the longest x1 22.2 us: decimate(): jnp.einsum('iqbw,wn->iqbn', window, lower, preferred_element_type=jnp.flo...]
    all_gather x2 -> x0, blocking collectives: 18.9 us -> none  [the longest x1 13.3 us: on_device(): piece = lax.all_gather(white_own, 'row', axis=0, tiled=True)]
    pallas_call x0 -> x2, Pallas kernels: none -> 18.7 us  [the longest x1 15.1 us: on_device(): pl.pallas_call(functools.partial(gather_kernel, nrows, ncols, slots, reco...]
    all_to_all x2 -> x0, starting transfers between devices: 11.4 us -> none  [the longest x1 6.32 us: on_device(): lax.all_to_all(labels, 'row', split_axis=0, concat_axis=0, tiled=True)]
    slice x4 -> x0, local copies, waits for them, and re-layouts: 7.24 us -> none  [the longest x2 3.9 us: decimate(): fir_taps[index]]
    dot_general x2 -> x0, local copies, waits for them, and re-layouts: 6.14 us -> none  [the longest x1 3.07 us: on_device(): jnp.einsum('ikb,jkb->ijb', left, right_real, preferred_element_type=jnp.f...]
    all_to_all x2 -> x0, waiting for transfers between devices: 5.41 us -> none  [the longest x1 5.41 us: on_device(): lax.all_to_all(outgoing, 'row', split_axis=0, concat_axis=0, tiled=True)]
    convert_element_type x4 -> x0, other arithmetic: 3.92 us -> none  [the longest x1 3.8 us: on_device(): (jnp.concatenate([real, imag], axis=2) / records).astype(jnp.bfloat16)]
  transfers between devices with their start and end apart: 2 -> 0, of which waited for: 1 -> 0; matrix products, arithmetic and copies ran while one was open for 54% -> 0% of each run, Pallas kernels for 0% -> 0%
where the time goes in v1:
time: 23.4 us; the launch traced here: 23.2 us
  Pallas kernels  18.7 us (80%)
  local copies, waits for them, and re-layouts  3.83 us (16%)
  between operations  0.67 us (3%)
    pallas_call x1, Pallas kernels, on_device(): pl.pallas_call(functools.partial(gather_kernel, nrows, ncols, slots, reco...  15.1 us
    unnamed x8, local copies, waits for them, and re-layouts  3.83 us
    pallas_call x1, Pallas kernels, on_device(): pl.pallas_call(functools.partial(pair_kernel, records), grid=(ncols,), ou...  3.63 us

profile of v1, /device:TPU:0, one launch (start us, length us, event | category | flops | bytes accessed | tf_op | source)
XLA Modules:
  0.0 23.2 jit_solution(2530955222831548439)
XLA Ops:
  0.7 0.0 copy-start
  0.7 1.9 %copy-done = bf16[16,1,8,12000]{3,2,1,0:T(8,128)(2,1)S(1)} copy-done((bf16[16,1,8,12000]{3,2,1,0:T(8,128)(2,1)S(1)}, bf16[16,1,8,12000]{3,2,1,0:T(8,128)(2,1)}, u32[]{:S(2)}) %copy-start) | copy-done | bytes 3072024
  2.5 0.0 copy-start.1
  2.5 0.7 %copy-done.1 = s32[16,1]{0,1:T(1,128)S(1)} copy-done((s32[16,1]{0,1:T(1,128)S(1)}, s32[16,1]{0,1:T(1,128)}, u32[]{:S(2)}) %copy-start.1) | copy-done | bytes 88
  3.2 0.0 copy-start.2
  3.2 0.7 %copy-done.2 = f32[32]{0:T(128)S(1)} copy-done((f32[32]{0:T(128)S(1)}, f32[32]{0:T(128)}, u32[]{:S(2)}) %copy-start.2) | copy-done | bytes 152
  3.8 0.0 copy-start.3
  3.8 0.7 %copy-done.3 = s32[64]{0:T(128)S(1)} copy-done((s32[64]{0:T(128)S(1)}, s32[64]{0:T(128)}, u32[]{:S(2)}) %copy-start.3) | copy-done | bytes 280
  4.5 15.1 %shard_map.55 = (bf16[8,64,128]{2,1,0:T(8,128)(2,1)S(1)}, bf16[4,8,16,128]{3,2,1,0:T(8,128)(2,1)S(1)}) custom-call(bf16[128,12000]{1,0:T(8,128)(2,1)S(1)} %bitcast.7, s32[16]{0:T(128)S(1)} %bitcast.8, s32[1]{0:T(128)} %bitcast.6.count_ref, f32[32]{0:T(128)S(1)} %copy-done.2, s32[64]{0:T(128)S(1)} %copy-done.3), custom_call_target="tpu_custom_call" | custom-call | tf_op jit(solution)/shard_map/pallas_call | solution.py:246
  19.6 3.6 %shard_map.56 = bf16[64,64,128]{2,1,0:T(8,128)(2,1)} custom-call(bf16[4,8,16,128]{3,2,1,0:T(8,128)(2,1)S(1)} %get-tuple-element.7.left_ref, bf16[8,64,128]{2,1,0:T(8,128)(2,1)S(1)} %get-tuple-element.8.right_ref), custom_call_target="tpu_custom_call" | custom-call | tf_op jit(solution)/shard_map/pallas_call | solution.py:275
Async XLA Ops:
  0.7 1.9 %copy-start = (bf16[16,1,8,12000]{3,2,1,0:T(8,128)(2,1)S(1)}, bf16[16,1,8,12000]{3,2,1,0:T(8,128)(2,1)}, u32[]{:S(2)}) copy-start(bf16[16,1,8,12000]{3,2,1,0:T(8,128)(2,1)} %param.5) | copy-start | bytes 9216004
  2.5 0.7 %copy-start.1 = (s32[16,1]{0,1:T(1,128)S(1)}, s32[16,1]{0,1:T(1,128)}, u32[]{:S(2)}) copy-start(s32[16,1]{0,1:T(1,128)} %param.6) | copy-start | bytes 196
  3.2 0.7 %copy-start.2 = (f32[32]{0:T(128)S(1)}, f32[32]{0:T(128)}, u32[]{:S(2)}) copy-start(f32[32]{0:T(128)} %fir_ref.1) | copy-start | bytes 388
  3.8 0.7 %copy-start.3 = (s32[64]{0:T(128)S(1)}, s32[64]{0:T(128)}, u32[]{:S(2)}) copy-start(s32[64]{0:T(128)} %bins_ref.1) | copy-start | bytes 772

commit v2 on v1

--- a/solution.py
+++ b/solution.py
@@ -30,10 +30,11 @@
 
 def gather_kernel(
     nrows, ncols, slots, records, samples, taps,
-    x_hbm, chan_ref, count_ref, fir_ref, bins_ref,
-    right_ref, left_ref,
-    x_ref, table_ref, edge_ref, cos_ref, sin_ref, white_ref, col_ref, label_ref,
-    load_sem, lsend, lrecv, rsend, rrecv, csend, crecv,
+    x_hbm, chan_hbm, count_hbm, fir_hbm, bins_hbm,
+    out_hbm,
+    chan_ref, count_ref, fir_ref, bins_ref, x_ref, table_ref, edge_ref, cos_ref, sin_ref, white_ref, col_ref, label_ref,
+    left_ref, u1_ref, u2_ref, v1_ref, v2_ref, block_ref,
+    store_sem, load_sem, small_sem, lsend, lrecv, rsend, rrecv, csend, crecv,
 ):
     me_row = lax.axis_index("row")
     me_col = lax.axis_index("col")
@@ -43,6 +44,12 @@
     for d in range(1, ncols):
         pl.semaphore_signal(barrier, inc=1, device_id={"col": lax.rem(me_col + d, ncols)}, device_id_type=MESH)
 
+    small = []
+    for n, (src, dst) in enumerate(
+        ((chan_hbm, chan_ref), (count_hbm, count_ref), (fir_hbm, fir_ref), (bins_hbm, bins_ref))
+    ):
+        small.append(pltpu.make_async_copy(src, dst, small_sem.at[n]))
+        small[-1].start()
     pieces = [(s, min(PIECE, samples - s)) for s in range(0, samples, PIECE)]
     loads = []
     for n, (start, size) in enumerate(pieces):
@@ -53,6 +60,8 @@
         loads.append(load)
 
     width = nrows * slots
+    for copy in small:
+        copy.wait()
     count = count_ref[0]
     lane = lax.broadcasted_iota(jnp.int32, (8, width), 1)
     label = jnp.full((8, width), -1, jnp.int32)
@@ -178,12 +187,19 @@
     pick = (wanted == label[0:1, :]).astype(F32).astype(BF16)
     for copy in row_copies:
         copy.wait()
+    wide = lax.broadcasted_iota(jnp.int32, (channels, LANES), 1) >= half
     for e in range(records):
         rows = jnp.concatenate([col_ref[r, e] for r in range(nrows)], axis=0)
-        right_ref[e] = jnp.dot(pick, rows, preferred_element_type=F32).astype(BF16)
+        v = jnp.dot(pick, rows, preferred_element_type=F32)
+        w = pltpu.roll(v, half, 1)
+        v1_ref[e] = jnp.where(wide, w, v)
+        v2_ref[e] = jnp.where(wide, v, w)
     first = pl.multiple_of(me_row * CH_DEV, CH_DEV)
+    own = lax.broadcasted_iota(jnp.int32, (CH_DEV, LANES), 1) >= half
     for e in range(records):
-        left_ref[me_col, e] = right_ref[e, pl.ds(first, CH_DEV), :]
+        v1 = v1_ref[e, pl.ds(first, CH_DEV), :]
+        v2 = v2_ref[e, pl.ds(first, CH_DEV), :]
+        left_ref[me_col, e] = jnp.where(own, v2, v1).astype(BF16)
     col_copies = []
     for d in range(1, ncols):
         copy = pltpu.make_async_remote_copy(
@@ -193,42 +209,41 @@
         )
         copy.start()
         col_copies.append(copy)
+    scale = 1.0 / records
+    stores = []
+    for d in range(ncols):
+        source = lax.rem(me_col + ncols - d, ncols)
+        if d > 0:
+            pltpu.make_async_remote_copy(
+                src_ref=left_ref.at[source], dst_ref=left_ref.at[source],
+                send_sem=csend.at[d], recv_sem=crecv.at[d],
+                device_id={"col": source}, device_id_type=MESH,
+            ).wait_recv()
+        for e in range(records):
+            u = left_ref[source, e].astype(F32) * scale
+            w = pltpu.roll(u, half, 1)
+            u1_ref[e] = u
+            u2_ref[e] = jnp.where(own, -w, w)
+
+        @pl.loop(0, channels // 16)
+        def _(jb):
+            at = pl.ds(pl.multiple_of(jb * 16, 16), 16)
+            v1 = [v1_ref[e, at, :] for e in range(records)]
+            v2 = [v2_ref[e, at, :] for e in range(records)]
+            for i in range(CH_DEV):
+                total = u1_ref[0, pl.ds(i, 1), :] * v1[0] + u2_ref[0, pl.ds(i, 1), :] * v2[0]
+                for e in range(1, records):
+                    total = total + u1_ref[e, pl.ds(i, 1), :] * v1[e]
+                    total = total + u2_ref[e, pl.ds(i, 1), :] * v2[e]
+                block_ref[source, i, at, :] = total.astype(BF16)
+
+        store = pltpu.make_async_copy(block_ref.at[source], out_hbm.at[source], store_sem.at[d])
+        store.start()
+        stores.append(store)
     for copy in col_copies:
-        copy.wait()
-
-
-def pair_kernel(records, left_ref, right_ref, out_ref, u1_ref, u2_ref, v1_ref, v2_ref):
-    half = LANES // 2
-    channels = right_ref.shape[1]
-
-    @pl.when(pl.program_id(0) == 0)
-    def _():
-        upper = lax.broadcasted_iota(jnp.int32, (channels, LANES), 1) >= half
-        for e in range(records):
-            v = right_ref[e].astype(F32)
-            w = pltpu.roll(v, half, 1)
-            v1_ref[e] = jnp.where(upper, w, v)
-            v2_ref[e] = jnp.where(upper, v, w)
-
-    upper = lax.broadcasted_iota(jnp.int32, (CH_DEV, LANES), 1) >= half
-    scale = 1.0 / records
-    for e in range(records):
-        u = left_ref[0, e].astype(F32) * scale
-        w = pltpu.roll(u, half, 1)
-        u1_ref[e] = u
-        u2_ref[e] = jnp.where(upper, -w, w)
-
-    @pl.loop(0, channels // 16)
-    def _(jb):
-        at = pl.ds(pl.multiple_of(jb * 16, 16), 16)
-        v1 = [v1_ref[e, at, :] for e in range(records)]
-        v2 = [v2_ref[e, at, :] for e in range(records)]
-        for i in range(CH_DEV):
-            total = u1_ref[0, pl.ds(i, 1), :] * v1[0] + u2_ref[0, pl.ds(i, 1), :] * v2[0]
-            for e in range(1, records):
-                total = total + u1_ref[e, pl.ds(i, 1), :] * v1[e]
-                total = total + u2_ref[e, pl.ds(i, 1), :] * v2[e]
-            out_ref[i, at, :] = total.astype(BF16)
+        copy.wait_send()
+    for store in stores:
+        store.wait()
 
 
 def on_device(raw_files, file_channels, reader_counts, fir_taps, band_bins):
@@ -241,17 +256,16 @@
     signal = raw_files.reshape(slots * records, samples)
     hop_rows = pl.cdiv(pl.cdiv(samples, SPAN), 8) * 8
     tall = SPAN // 8 + hop_rows
-    smem = pl.BlockSpec(memory_space=pltpu.SMEM)
-    vmem = pl.BlockSpec(memory_space=pltpu.VMEM)
-    right, left = pl.pallas_call(
+    stacked = pl.pallas_call(
         functools.partial(gather_kernel, nrows, ncols, slots, records, samples, taps),
-        out_shape=(
-            jax.ShapeDtypeStruct((records, channels, LANES), BF16),
-            jax.ShapeDtypeStruct((ncols, records, CH_DEV, LANES), BF16),
-        ),
-        in_specs=[pl.BlockSpec(memory_space=pl.ANY), smem, smem, smem, smem],
-        out_specs=(vmem, vmem),
+        out_shape=jax.ShapeDtypeStruct((ncols, CH_DEV, channels, LANES), BF16),
+        in_specs=[pl.BlockSpec(memory_space=pltpu.HBM)] * 5,
+        out_specs=pl.BlockSpec(memory_space=pltpu.HBM),
         scratch_shapes=[
+            pltpu.SMEM((slots,), jnp.int32),
+            pltpu.SMEM((1,), jnp.int32),
+            pltpu.SMEM(fir_taps.shape, F32),
+            pltpu.SMEM(band_bins.shape, jnp.int32),
             pltpu.VMEM((slots * records, samples), BF16),
             pltpu.VMEM((SPAN, 2 * LANES), BF16),
             pltpu.VMEM((LANES, LANES), BF16),
@@ -260,7 +274,15 @@
             pltpu.VMEM((slots * records, LANES), F32),
             pltpu.VMEM((nrows, records, slots, LANES), BF16),
             pltpu.VMEM((nrows, 8, width), jnp.int32),
+            pltpu.VMEM((ncols, records, CH_DEV, LANES), BF16),
+            pltpu.VMEM((records, CH_DEV, LANES), F32),
+            pltpu.VMEM((records, CH_DEV, LANES), F32),
+            pltpu.VMEM((records, channels, LANES), F32),
+            pltpu.VMEM((records, channels, LANES), F32),
+            pltpu.VMEM((ncols, CH_DEV, channels, LANES), BF16),
+            pltpu.SemaphoreType.DMA((ncols,)),
             pltpu.SemaphoreType.DMA((pl.cdiv(samples, PIECE),)),
+            pltpu.SemaphoreType.DMA((4,)),
             pltpu.SemaphoreType.DMA((nrows,)),
             pltpu.SemaphoreType.DMA((nrows,)),
             pltpu.SemaphoreType.DMA((nrows,)),
@@ -269,27 +291,10 @@
             pltpu.SemaphoreType.DMA((ncols,)),
         ],
         compiler_params=pltpu.CompilerParams(
-            collective_id=0, has_side_effects=True, vmem_limit_bytes=40 * 2**20
+            collective_id=0, has_side_effects=True, vmem_limit_bytes=60 * 2**20
         ),
     )(signal, file_channels.reshape(-1), reader_counts.reshape(-1), fir_taps, band_bins)
-    stacked = pl.pallas_call(
-        functools.partial(pair_kernel, records),
-        grid=(ncols,),
-        out_shape=jax.ShapeDtypeStruct((ncols * CH_DEV, channels, LANES), BF16),
-        in_specs=[
-            pl.BlockSpec((1, records, CH_DEV, LANES), lambda c: (c, 0, 0, 0)),
-            pl.BlockSpec((records, channels, LANES), lambda c: (0, 0, 0)),
-        ],
-        out_specs=pl.BlockSpec((CH_DEV, channels, LANES), lambda c: (c, 0, 0)),
-        scratch_shapes=[
-            pltpu.VMEM((records, CH_DEV, LANES), F32),
-            pltpu.VMEM((records, CH_DEV, LANES), F32),
-            pltpu.VMEM((records, channels, LANES), F32),
-            pltpu.VMEM((records, channels, LANES), F32),
-        ],
-        compiler_params=pltpu.CompilerParams(vmem_limit_bytes=40 * 2**20),
-    )(left, right)
-    return stacked[:, None, :, :]
+    return stacked.reshape(ncols * CH_DEV, 1, channels, LANES)
 
 
 def solution(mesh):

time: 23.4 us -> 19.9 us (0.85)
  Pallas kernels: 18.7 us -> 16.8 us
  local copies, waits for them, and re-layouts: 3.83 us -> 2.26 us
    pallas_call x1 -> x0, Pallas kernels: 3.63 us -> none  [on_device(): pl.pallas_call(functools.partial(pair_kernel, records), grid=(ncols,), ou...]
    pallas_call x1, Pallas kernels: 15.1 us -> 16.8 us  [on_device(): pl.pallas_call(functools.partial(gather_kernel, nrows, ncols, slots, reco...]
    unnamed x8 -> x1, local copies, waits for them, and re-layouts: 3.83 us -> 2.26 us
where the time goes in v2:
time: 19.9 us; the launch traced here: 19.8 us
  Pallas kernels  16.8 us (84%)
  local copies, waits for them, and re-layouts  2.26 us (11%)
  between operations  0.66 us (3%)
    pallas_call x1, Pallas kernels, on_device(): pl.pallas_call(functools.partial(gather_kernel, nrows, ncols, slots, reco...  16.8 us
    unnamed x1, local copies, waits for them, and re-layouts  2.26 us

profile of v2, /device:TPU:0, one launch (start us, length us, event | category | flops | bytes accessed | tf_op | source)
XLA Modules:
  0.0 19.8 jit_solution(5961905757300544785)
XLA Ops:
  0.7 16.8 %shard_map.55 = bf16[4,16,64,128]{3,2,1,0:T(8,128)(2,1)} custom-call(bf16[128,12000]{1,0:T(8,128)(2,1)} %bitcast.8, s32[16]{0:T(128)} %bitcast.9, s32[1]{0:T(128)} %bitcast.6.count_hbm, f32[32]{0:T(128)} %fir_hbm.1, s32[64]{0:T(128)} %bins_hbm.1), custom_call_target="tpu_custom_call" | custom-call | tf_op jit(solution)/shard_map/pallas_call | solution.py:259
  17.5 2.3 %copy.9 = bf16[64,1,64,128]{3,2,1,0:T(8,128)(2,1)} copy(bf16[64,1,64,128]{3,2,1,0:T(8,128)(2,1)} %bitcast.7) | data formatting | bytes 2097152
